TPU v7x, 32 devices: a whole 2x2x4 slice. The times are simulated.
32 devices in a mesh: gx: 8 (over z, x), gy: 4 (over y, core).
Axes of the slice: x: 2, y: 2, z: 4, core: 2. Of those that a mesh axis runs over, the one named last changes fastest.
Arguments:
- conc: float32 [64, 128, 256], P('gx', 'gy'), may hold values from 0 to 1
- labels: int32 [64, 128, 256], P('gx', 'gy'), may hold values from 0 to 2
- kappa: float32 [3], replicated, may hold values from 0.1 to 1
- adjoint_source: float32 [64, 128, 256], P('gx', 'gy'), may hold values from -40 to 40
Outputs:
- adjoint: float32 [64, 128, 256], P('gx', 'gy')
- residual: float32 [64, 128, 256], P('gx', 'gy')
All inputs are finite; a program needn't handle non-finite values.
Results may differ from a plain program's by a relative error of at most 0.008.
Values sent between devices are 32-bit elements; how exact they have to be, the bound alone decides.
No kernel may reach another device: no remote copies, remote signals or barrier semaphores. Data moves between devices by JAX's collectives and lax.ppermute only.
A program may use at most 64 MiB of HBM per device.

v0:
```python
import functools

import jax
import jax.numpy as jnp
from jax import lax
from jax.experimental import pallas as pl
from jax.experimental.pallas import tpu as pltpu
from jax.sharding import PartitionSpec as P

ITERS = 2
DT = 0.5
W = 2 * ITERS
F32 = jnp.float32
LANES = 128
YROWS = (8, 8)
VMEM = pl.BlockSpec(memory_space=pltpu.VMEM)


def low_first(axis):
    return lax.axis_index(axis) % 2 == 0


def up(v, axis):
    return pltpu.roll(v, v.shape[axis] - 1, axis)


def down(v, axis):
    return pltpu.roll(v, 1, axis)


def z_ends(shape):
    index = lax.broadcasted_iota(jnp.int32, shape, 1)
    return index == 0, index == shape[1] - 1


def coupling(u, d, un, dn):
    return d + d * u - d * un + dn


def params(megabytes=16):
    return pltpu.CompilerParams(vmem_limit_bytes=megabytes << 20)


def f32(*shape):
    return jax.ShapeDtypeStruct(shape, F32)


FIELDS = 7


def late_rows(ny):
    rows = ny + 2 * W
    for field, n in ((0, 3), (1, 3), (2, 3), (3, 2), (4, 1), (5, 1)):
        yield field, ny, n
        yield field, rows - n, n
    for field, n in ((5, 1), (6, 2)):
        yield field, 0, n
        yield field, ny - n, n


def late_count(ny):
    return sum(n for _, _, n in late_rows(ny))


def pack_kernel(
    kappa_in, conc_in, labels_in, source_in,
    conc, source, diff,
    labels, kappa, sems,
):
    nx, ny, nz = conc.shape
    copies = [
        pltpu.make_async_copy(src, dst, sems.at[k])
        for k, (src, dst) in enumerate(
            (
                (labels_in, labels),
                (conc_in, conc),
                (kappa_in, kappa),
                (source_in, source),
            )
        )
    ]
    for copy in copies:
        copy.start()
    for copy in copies[:3]:
        copy.wait()
    k0, k1, k2 = ((0.5 * DT) * kappa[k] for k in range(3))

    def body(x, carry):
        lab = labels[x]
        base = jnp.where(lab == 0, k0, jnp.where(lab == 1, k1, k2))
        diff[x] = base * jnp.exp(conc[x])
        return carry

    lax.fori_loop(0, nx, body, 0, unroll=True)
    copies[3].wait()


def pack(conc, labels, kappa, source):
    nx, ny, nz = conc.shape
    outside = [
        pltpu.with_memory_space_constraint(v, pltpu.HBM)
        for v in (kappa, conc, labels, source)
    ]
    return pl.pallas_call(
        pack_kernel,
        out_shape=(f32(nx, ny, nz),) * 3,
        in_specs=[pl.BlockSpec(memory_space=pltpu.HBM)] * 4,
        out_specs=(VMEM,) * 3,
        scratch_shapes=[
            pltpu.VMEM((nx, ny, nz), jnp.int32),
            pltpu.SMEM((3,), F32),
            pltpu.SemaphoreType.DMA((4,)),
        ],
        compiler_params=params(),
        name="pack",
    )(*outside)


def pack_rows_kernel(conc, diff, source, yone, ytwo):
    nx, ny, nz = conc.shape
    flip = low_first("gy")
    for k, ref in enumerate((conc, diff, source)):
        for out, n, head in ((yone, YROWS[0], flip), (ytwo, YROWS[1], ~flip)):
            out[k, 0:nx] = jnp.where(head, ref[:, 0:n, :], ref[:, ny - n : ny, :])
        yone[k, nx] = jnp.zeros((YROWS[0], nz), F32)


def pack_rows(conc, diff, source):
    nx, ny, nz = conc.shape
    return pl.pallas_call(
        pack_rows_kernel,
        out_shape=(f32(3, nx + 1, YROWS[0], nz), f32(3, nx, YROWS[1], nz)),
        in_specs=[VMEM] * 3,
        out_specs=(VMEM,) * 2,
        compiler_params=params(),
        name="pack_rows",
    )(conc, diff, source)


def rows_beside(yone, ytwo, k, x):
    flip = low_first("gy")
    one, two = (slice(n - W, n) for n in YROWS)
    below = jnp.where(flip, yone[k, x, one], ytwo[k, x, two])
    return below, jnp.where(flip, ytwo[k, x, 0:W], yone[k, x, 0:W])


def in_plane_adjoint(v, fy, gy, fz, gz):
    total = fy * up(v, 0) + gy * down(v, 0)
    return total + (fz * up(v, 1) + gz * down(v, 1))


def in_plane_forward(v, fy, gy, fz, gz):
    total = up(gy * v, 0) + down(fy * v, 0)
    return total + (up(gz * v, 1) + down(fz * v, 1))


def in_plane_couplings(u, d):
    first, last = z_ends(u.shape)
    fy = coupling(u, d, up(u, 0), up(d, 0))
    gy = coupling(u, d, down(u, 0), down(d, 0))
    fz = coupling(u, d, jnp.where(last, 0.0, up(u, 1)), jnp.where(last, 0.0, up(d, 1)))
    gz = coupling(
        u, d, jnp.where(first, 0.0, down(u, 1)), jnp.where(first, 0.0, down(d, 1))
    )
    return fy, gy, fz, gz


def face_planes(first_swap, nx):
    at_head = low_first("gx") if first_swap else ~low_first("gx")
    return [jnp.where(at_head, k, nx - 1 - k) for k in range(4)]


def face_fields(u, d, s):
    first, last = z_ends(u[0].shape)

    def between(i, j):
        return coupling(u[i], d[i], u[j], d[j])

    def image(i, before, after):
        fy, gy, fz, gz = in_plane_couplings(u[i], d[i])
        diagonal = 1.0 + ((fy + gy) + (fz + gz)) + (before + after)
        beside = (fy, gy, jnp.where(last, 0.0, fz), jnp.where(first, 0.0, gz))
        total = diagonal * s[i] - before * s[i - 1] - after * s[i + 1]
        total = total - in_plane_adjoint(s[i], *beside)
        return jnp.where(d[i] > 0.0, total, 0.0), diagonal, beside

    back, inward = between(1, 0), between(2, 1)
    near, diagonal, beside = image(1, back, between(1, 2))
    far, _, _ = image(2, inward, between(2, 3))
    rest = diagonal * near - inward * far - in_plane_forward(near, *beside)
    return u[0], d[0], s[0], s[1], between(0, 1), back * near, rest


def face_rows(first_swap, ny):
    return FIELDS * ny + (-1 if first_swap else 1)


def pack_face_kernel(first_swap, conc, diff, source, slab):
    nx, ny, nz = conc.shape
    planes = face_planes(first_swap, nx)
    u, d, s = ([ref[x] for x in planes] for ref in (conc, diff, source))
    for k, v in enumerate(face_fields(u, d, s)):
        n = min(ny, slab.shape[0] - k * ny)
        slab[k * ny : k * ny + n] = v[0:n]
    if not first_swap:
        slab[FIELDS * ny :] = jnp.zeros((1, nz), F32)


def pack_face(first_swap, conc, diff, source):
    _, ny, nz = conc.shape
    return pl.pallas_call(
        functools.partial(pack_face_kernel, first_swap),
        out_shape=f32(face_rows(first_swap, ny), nz),
        in_specs=[VMEM] * 3,
        out_specs=VMEM,
        compiler_params=params(),
        name="pack_face",
    )(conc, diff, source)


def pack_late_kernel(
    conc, diff, source, yone, ytwo, cone, ctwo, near_s, out_s
):
    nx, ny, nz = conc.shape
    rows = ny + 2 * W

    def narrow(row):
        if row < ny:
            return row + W if row < W else row - ny + 3 * W
        return row - ny + 3 * W if row < ny + W else row - ny - W

    for first_swap, late in ((True, cone), (False, ctwo)):
        for j, x in enumerate(face_planes(first_swap, nx)):
            for k, ref in enumerate((conc, diff, source)):
                below, above = rows_beside(yone, ytwo, k, x)
                near_s[k, j, 0:W] = below
                near_s[k, j, W : 2 * W] = ref[x, 0:W]
                near_s[k, j, 2 * W : 3 * W] = ref[x, ny - W : ny]
                near_s[k, j, 3 * W :] = above
        fields = face_fields(*([near_s[k, j] for j in range(4)] for k in range(3)))
        for k, v in enumerate(fields):
            out_s[k] = v
        for at in (W - 2, 3 * W + 1):
            mine, following, k = (out_s[j, at : at + 1] for j in (2, 3, 4))
            out_s[3, at : at + 1] = mine - k * (mine - following)
        row = 0
        for k, begin, n in late_rows(ny):
            at = narrow(begin)
            late[row : row + n] = out_s[k, at : at + n]
            row += n


def pack_late(conc, diff, source, yone, ytwo):
    nx, ny, nz = conc.shape
    return pl.pallas_call(
        pack_late_kernel,
        out_shape=(f32(late_count(ny), nz),) * 2,
        in_specs=[VMEM] * 5,
        out_specs=(VMEM,) * 2,
        scratch_shapes=[
            pltpu.VMEM((3, 4, 4 * W, nz), F32),
            pltpu.VMEM((FIELDS, 4 * W, nz), F32),
        ],
        compiler_params=params(),
        name="pack_late",
    )(conc, diff, source, yone, ytwo)


def own_kernel(
    conc, diff, source, yone, ytwo,
    u_s, d_s, s_s, fx, gx, fy, gy, fz, gz, dg, p1,
):
    nx, ny, nz = conc.shape
    rows = ny + 2 * W
    for k, (own, ref) in enumerate(((conc, u_s), (diff, d_s), (source, s_s))):
        below, above = rows_beside(yone, ytwo, k, slice(0, nx))
        ref[:, 0:ny, :] = own[...]
        ref[:, ny : ny + W, :] = above
        ref[:, ny + W :, :] = below
    first, last = z_ends((rows, nz))

    for q in range(nx):
        u, d = u_s[q], d_s[q]
        fyq, gyq, fzq, gzq = in_plane_couplings(u, d)
        total = 1.0 + ((fyq + gyq) + (fzq + gzq))
        if q + 1 < nx:
            fxq = coupling(u, d, u_s[q + 1], d_s[q + 1])
            fx[q] = fxq
            total = total + fxq
        if q > 0:
            gxq = coupling(u, d, u_s[q - 1], d_s[q - 1])
            gx[q] = gxq
            total = total + gxq
        dg[q] = total
        fy[q] = fyq
        gy[q] = gyq
        fz[q] = jnp.where(last, 0.0, fzq)
        gz[q] = jnp.where(first, 0.0, gzq)

    for q in range(1, nx - 1):
        v = s_s[q]
        total = dg[q] * v - fx[q] * s_s[q + 1] - gx[q] * s_s[q - 1]
        total = total - in_plane_adjoint(v, fy[q], gy[q], fz[q], gz[q])
        p1[q] = jnp.where(d_s[q] > 0.0, total, 0.0)


def own(conc, diff, source, yone, ytwo):
    nx, ny, nz = conc.shape
    return pl.pallas_call(
        own_kernel,
        out_shape=(f32(nx, ny + 2 * W, nz),) * 11,
        in_specs=[VMEM] * 5,
        out_specs=(VMEM,) * 11,
        compiler_params=params(),
        name="own",
    )(conc, diff, source, yone, ytwo)


def mask_halo(total, d, ny):
    return jnp.concatenate([total[0:ny], jnp.where(d > 0.0, total[ny:], 0.0)], axis=0)


def product(v, w, ny):
    both = v[0:ny] * w[0:ny]
    return jnp.sum(both.reshape(ny // 8, 8, both.shape[1]), axis=0)


def ratio(over, under, whole):
    over, under, whole = (
        jnp.sum(v, axis=(0, 1), keepdims=True) for v in (over, under, whole)
    )
    under = jnp.where(whole <= 16.0 * under, under, whole)
    return jnp.where(under > 0.0, over / jnp.where(under > 0.0, under, 1.0), 0.0)


SUMS = 6


def inside_kernel(d_s, s_s, fx, gx, fy, gy, fz, gz, dg, p1, p2, p3, part):
    nx, rows, nz = d_s.shape
    ny = rows - 2 * W
    sums = [jnp.zeros((8, nz), F32) for _ in range(SUMS)]
    over, under = jnp.zeros((8, nz), F32), jnp.zeros((8, nz), F32)
    for q in range(nx):
        sums[0] = sums[0] + product(s_s[q], s_s[q], ny)
    for q in range(1, nx - 1):
        sums[1] = sums[1] + product(p1[q], p1[q], ny)
    for q in range(2, nx - 2):
        v = p1[q]
        total = dg[q] * v - gx[q + 1] * p1[q + 1] - fx[q - 1] * p1[q - 1]
        total = total - in_plane_forward(v, fy[q], gy[q], fz[q], gz[q])
        p2[q] = jnp.where(d_s[q] > 0.0, total, 0.0)
        over = over + product(total, s_s[q], ny)
        under = under + product(s_s[q], s_s[q], ny)
    theta = ratio(over, under, sums[0])
    for q in range(2, nx - 2):
        v = p2[q] - theta * s_s[q]
        sums[2] = sums[2] + product(s_s[q], v, ny)
        sums[3] = sums[3] + product(v, v, ny)
    over, under = jnp.zeros((8, nz), F32), jnp.zeros((8, nz), F32)
    for q in range(3, nx - 3):
        v = p2[q]
        total = dg[q] * v - fx[q] * p2[q + 1] - gx[q] * p2[q - 1]
        total = total - in_plane_adjoint(v, fy[q], gy[q], fz[q], gz[q])
        p3[q] = jnp.where(d_s[q] > 0.0, total, 0.0)
        over = over + product(total, p1[q], ny)
        under = under + product(p1[q], p1[q], ny)
    phi = ratio(over, under, sums[1])
    for q in range(3, nx - 3):
        w = p3[q] - phi * p1[q]
        sums[4] = sums[4] + product(p1[q], w, ny)
        sums[5] = sums[5] + product(w, w, ny)
    for k, total in enumerate(sums):
        part[k] = total
    part[SUMS] = jnp.broadcast_to(theta, (8, nz))
    part[SUMS + 1] = jnp.broadcast_to(phi, (8, nz))


def inside(d_s, *fields):
    nx, rows, nz = d_s.shape
    return pl.pallas_call(
        inside_kernel,
        out_shape=(f32(nx, rows, nz),) * 2 + (f32(SUMS + 2, 8, nz),),
        in_specs=[VMEM] * 10,
        out_specs=(VMEM,) * 3,
        compiler_params=params(),
        cost_estimate=pl.CostEstimate(
            flops=1 << 22, bytes_accessed=1 << 23, transcendentals=0
        ),
        name="inside",
    )(d_s, *fields)


def finish_kernel(
    u_s, d_s, s_s, fx, gx, fy, gy, fz, gz, dg, p1_in, p2_in, p3_in, part,
    xtwo, xone, ctwo, cone,
    p1_out, p2_out, p3_out, edge_s, moments,
    side_s, w_s,
):
    nx, rows, nz = d_s.shape
    ny = rows - 2 * W
    flip = low_first("gx")
    first, last = z_ends((rows, nz))

    for side, one in ((0, flip), (1, ~flip)):
        for k in range(FIELDS):
            n = min(ny, xone.shape[0] - k * ny)
            held = slice(k * ny, k * ny + n)
            side_s[side, k, 0:n] = jnp.where(one, xone[held], xtwo[held])
        side_s[side, :, ny:] = jnp.zeros((FIELDS, 2 * W, nz), F32)
        for at in (ny + 1, rows - 2):
            side_s[side, 4, at : at + 1] = jnp.ones((1, nz), F32)
        late = jnp.where(one, cone[...], ctwo[...])
        row = 0
        for field, begin, n in late_rows(ny):
            side_s[side, field, begin : begin + n] = late[row : row + n]
            row += n

    names = dict(
        u=u_s, d=d_s, s=s_s, fx=fx, gx=gx, fy=fy, gy=gy, fz=fz, gz=gz, dg=dg,
        p1=p1_in, p2=p2_in, p3=p3_in,
    )
    place = {(k, q): names[k].at[q] for k in names for q in range(nx)}
    spare = iter(range(w_s.shape[0]))

    def keep(name, q, value):
        place[name, q] = w_s.at[next(spare)]
        place[name, q][...] = value

    def get(name, q):
        return place[name, q][...]

    for side, (o, e, outward, inward) in enumerate(
        ((-1, 0, "gx", "fx"), (nx, nx - 1, "fx", "gx"))
    ):
        beyond = 2 * o - e
        for k, name in enumerate(("u", "d", "s")):
            place[name, o] = side_s.at[side, k]
        place["s", beyond] = side_s.at[side, 3]
        place[outward, o] = side_s.at[side, 4]
        place["m", o] = side_s.at[side, 5]
        place["q", o] = side_s.at[side, 6]
        u, d, ue, de = get("u", o), get("d", o), get("u", e), get("d", e)
        back = coupling(u, d, ue, de)
        out = coupling(ue, de, u, d)
        fyq, gyq, fzq, gzq = in_plane_couplings(u, d)
        total = 1.0 + get(outward, o) + back + ((fyq + gyq) + (fzq + gzq))
        new = {
            (inward, o): back,
            (outward, e): out,
            ("dg", o): total,
            ("dg", e): get("dg", e) + out,
            ("fy", o): fyq,
            ("gy", o): gyq,
            ("fz", o): jnp.where(last, 0.0, fzq),
            ("gz", o): jnp.where(first, 0.0, gzq),
        }
        for k, (key, value) in enumerate(new.items()):
            place[key] = edge_s.at[side, k]
            place[key][...] = value

    def masked(total, q):
        if q in (-1, nx):
            return jnp.where(get("d", q) > 0.0, total, 0.0)
        return mask_halo(total, place["d", q][ny:], ny)

    def in_plane(q):
        return [get(k, q) for k in ("fy", "gy", "fz", "gz")]

    def adjoint_at(w, q):
        v = get(w, q)
        total = get("dg", q) * v - get("fx", q) * get(w, q + 1)
        total = total - get("gx", q) * get(w, q - 1)
        return masked(total - in_plane_adjoint(v, *in_plane(q)), q)

    def forward_at(w, q):
        v = get(w, q)
        above = get("m", q) if q == nx else get("gx", q + 1) * get(w, q + 1)
        below = get("m", q) if q == -1 else get("fx", q - 1) * get(w, q - 1)
        total = get("dg", q) * v - above - below
        return masked(total - in_plane_forward(v, *in_plane(q)), q)

    sums = [part[k] for k in range(SUMS)]
    theta, phi = (part[SUMS + k][0:1, 0:1] for k in range(2))

    def add(k, v, w):
        sums[k] = sums[k] + product(v, w, ny)

    for q in range(-1, nx + 1):
        if 1 <= q < nx - 1:
            continue
        value = adjoint_at("s", q)
        keep("p1", q, value)
        if 0 <= q < nx:
            p1_out[q] = value[0:ny]
            add(1, value, value)
    for q in range(-1, nx + 1):
        if 2 <= q < nx - 2:
            continue
        value = forward_at("p1", q)
        keep("p2", q, value)
        if 0 <= q < nx:
            p2_out[q] = value[0:ny]
            v = value - theta * get("s", q)
            add(2, get("s", q), v)
            add(3, v, v)
    for o, outward in ((-1, "gx"), (nx, "fx")):
        beyond = -2 if o == -1 else nx + 1
        keep("p2", beyond, get("q", o) - get(outward, o) * get("p1", o))
    for q in range(-1, nx + 1):
        if 3 <= q < nx - 3:
            continue
        value = adjoint_at("p2", q)
        p3_out[q + 1] = value
        if 0 <= q < nx:
            w = value - phi * get("p1", q)
            add(4, get("p1", q), w)
            add(5, w, w)

    slot = lax.broadcasted_iota(jnp.int32, (1, LANES), 1)
    row = jnp.where(slot == SUMS, theta, phi)
    for k in range(SUMS):
        total = jnp.sum(sums[k], axis=0, keepdims=True)
        total = jnp.sum(total, axis=1, keepdims=True)
        row = jnp.where(slot == k, total, row)
    moments[...] = jnp.broadcast_to(row, moments.shape)


def finish(copies, ny, *fields):
    nx, rows, nz = fields[0].shape
    steps = 4 + 6 + 2
    return pl.pallas_call(
        finish_kernel,
        out_shape=(
            f32(nx, ny, nz),
            f32(nx, ny, nz),
            f32(nx + 2, rows, nz),
            f32(2, 8, rows, nz),
            f32(copies, 1, LANES),
        ),
        in_specs=[VMEM] * len(fields),
        out_specs=(VMEM,) * 5,
        scratch_shapes=[
            pltpu.VMEM((2, FIELDS, rows, nz), F32),
            pltpu.VMEM((steps, rows, nz), F32),
        ],
        compiler_params=params(),
        name="finish",
    )(*fields)


def combine_kernel(
    moments, source, p1_in, p2_in, p3_in, p1_out, p2_out, p3_out, edge,
    fx, gx, fy, gy, fz, gz, dg,
    adjoint_out, residual_out,
    adjoint, residual, sems,
):
    nx, ny, nz = source.shape
    p1 = [(p1_in if 1 <= x < nx - 1 else p1_out).at[x] for x in range(nx)]
    p2 = [(p2_in if 2 <= x < nx - 2 else p2_out).at[x] for x in range(nx)]
    p3 = [
        p3_in.at[x] if 3 <= x < nx - 3 else p3_out.at[x + 1] for x in range(-1, nx + 1)
    ]
    sums = [moments[:, k : k + 1] for k in range(SUMS + 2)]
    ss, pp, sv, vv, pw, ww, theta, phi = sums

    def total(v):
        return jnp.sum(v, axis=0, keepdims=True)

    def norm(g, a, shift, first, mixed, second):
        rest = g - a * shift
        return total(rest * rest * first - 2.0 * a * rest * mixed + a * a * second)

    m0 = total(ss)
    alpha = m0 / total(pp)
    new = norm(1.0, alpha, theta, ss, sv, vv)
    grow = 1.0 + new / m0
    step = new / norm(grow, alpha, phi, pp, pw, ww)
    near = alpha + step * grow
    far = step * alpha
    copies = []

    def send(src, dst, begin, end):
        planes = pl.ds(begin, end - begin)
        copies.append(
            pltpu.make_async_copy(src.at[planes], dst.at[planes], sems.at[len(copies)])
        )
        copies[-1].start()

    half = nx // 2
    for begin in (0, half):
        for x in range(begin, begin + half):
            adjoint[x] = near * p1[x][0:ny] - far * p3[x + 1][0:ny]
        send(adjoint, adjoint_out, begin, begin + half)
    for x in range(nx):
        v = p3[x + 1][...]
        above = edge[1, 0] if x == nx - 1 else gx[x + 1]
        below = edge[0, 0] if x == 0 else fx[x - 1]
        diagonal = edge[0, 3] if x == 0 else edge[1, 3] if x == nx - 1 else dg[x]
        p4 = diagonal * v - above * p3[x + 2][...] - below * p3[x][...]
        p4 = p4 - in_plane_forward(v, fy[x], gy[x], fz[x], gz[x])
        residual[x] = source[x] - near * p2[x][0:ny] + far * p4[0:ny]
        if x % 2 == 1:
            send(residual, residual_out, x - 1, x + 1)
    for copy in copies:
        copy.wait()


def combine(moments, source, *fields):
    nx, ny, nz = source.shape
    return pl.pallas_call(
        combine_kernel,
        out_shape=(f32(nx, ny, nz),) * 2,
        in_specs=[VMEM] * (2 + len(fields)),
        out_specs=(pl.BlockSpec(memory_space=pltpu.HBM),) * 2,
        scratch_shapes=[
            pltpu.VMEM((nx, ny, nz), F32),
            pltpu.VMEM((nx, ny, nz), F32),
            pltpu.SemaphoreType.DMA((2 + nx // 2,)),
        ],
        compiler_params=params(),
        name="combine",
    )(moments, source, *fields)


def swap(cells, axis, first):
    pairs = [(i, i + 1) for i in range(first, lax.axis_size(axis) - 1, 2)]
    return lax.ppermute(cells, axis, pairs + [(j, i) for i, j in pairs])


def local(conc, labels, kappa, source):
    ny = conc.shape[1]
    conc, source, diff = pack(conc, labels, kappa, source)
    xtwo = swap(pack_face(False, conc, diff, source), "gx", 0)
    xone = swap(pack_face(True, conc, diff, source), "gx", 1)
    yone, ytwo = pack_rows(conc, diff, source)
    yone = swap(yone, "gy", 1)
    ytwo = swap(ytwo, "gy", 0)
    cone, ctwo = pack_late(conc, diff, source, yone, ytwo)
    ctwo = swap(ctwo, "gx", 0)
    cone = swap(cone, "gx", 1)
    fields = own(conc, diff, source, yone, ytwo)
    inner = inside(*fields[1:])
    p1, p2, p3, edge, moments = finish(
        lax.axis_size(("gx", "gy")), ny, *fields, *inner, xtwo, xone, ctwo, cone
    )
    moments = lax.all_to_all(moments, ("gx", "gy"), 0, 0, tiled=True)
    moments = moments.reshape(-1, LANES)
    return combine(
        moments, source, fields[10], *inner[:2], p1, p2, p3, edge, *fields[3:10]
    )


def solution(mesh):
    return jax.shard_map(
        local,
        mesh=mesh,
        in_specs=(P("gx", "gy", None), P("gx", "gy", None), P(), P("gx", "gy", None)),
        out_specs=(P("gx", "gy", None), P("gx", "gy", None)),
        check_vma=False,
    )
```

profile of v0, /device:TPU:0, one launch (start us, length us, event | category | flops | bytes accessed | tf_op | source)
XLA Modules:
  0.0 33.1 jit_solution(10420976550801534971)
XLA Ops:
  0.6 1.1 %pack.1 = (f32[8,32,256]{2,1,0:T(8,128)S(1)}, f32[8,32,256]{2,1,0:T(8,128)S(1)}, f32[8,32,256]{2,1,0:T(8,128)S(1)}) custom-call(f32[3]{0:T(128)} %kappa_in.1, f32[8,32,256]{2,1,0:T(8,128)} %conc_in.1, s32[8,32,256]{2,1,0:T(8,128)} %labels_in.1, f32[8,32,256]{2,1,0:T(8,128)} %source_in.1), custom_call_target="tpu_custom_call" | custom-call | tf_op jit(solution)/shard_map/pack/pallas_call | solution.py:104
  1.8 0.7 %collective-permute-start = (f32[3,9,8,256]{3,2,1,0:T(8,128)S(1)}, f32[3,9,8,256]{3,2,1,0:T(8,128)S(1)}, u32[]{:S(2)}, u32[]{:S(2)}) collective-permute-start(f32[3,9,8,256]{3,2,1,0:T(8,128)S(1)} %get-tuple-element.31), channel_id=1, source_target_pairs={{1,2},{2,1},{5,6},{6,5},{9,10},{10,9},{13,14},{14,13},{17,18},{18,... | collective-permute-start | bytes 663560 | tf_op jit(solution)/shard_map/ppermute | solution.py:628
  2.5 0.2 pack_face.2
  2.8 3.0 %collective-permute-start.2 = (f32[225,256]{1,0:T(8,128)S(1)}, f32[225,256]{1,0:T(8,128)S(1)}, u32[]{:S(2)}, u32[]{:S(2)}) collective-permute-start(f32[225,256]{1,0:T(8,128)S(1)} %pack_face.2), channel_id=1, source_target_pairs={{0,4},{8,12},{16,20},{24,28},{4,0},{12,8},{20,16},{28,24},{1,5},{9... | collective-permute-start | bytes 691208 | tf_op jit(solution)/shard_map/ppermute | solution.py:628
  5.8 2.6 %collective-permute-start.1 = (f32[3,8,8,256]{3,2,1,0:T(8,128)S(1)}, f32[3,8,8,256]{3,2,1,0:T(8,128)S(1)}, u32[]{:S(2)}, u32[]{:S(2)}) collective-permute-start(f32[3,8,8,256]{3,2,1,0:T(8,128)S(1)} %get-tuple-element.32), channel_id=1, source_target_pairs={{0,1},{2,3},{1,0},{3,2},{4,5},{6,7},{5,4},{7,6},{8,9},{10,11},{9,8... | collective-permute-start | bytes 589832 | tf_op jit(solution)/shard_map/ppermute | solution.py:628
  8.3 0.2 pack_face.3
  8.6 0.7 %collective-permute-start.3 = (f32[223,256]{1,0:T(8,128)S(1)}, f32[223,256]{1,0:T(8,128)S(1)}, u32[]{:S(2)}, u32[]{:S(2)}) collective-permute-start(f32[223,256]{1,0:T(8,128)S(1)} %pack_face.3), channel_id=1, source_target_pairs={{4,8},{12,16},{20,24},{8,4},{16,12},{24,20},{5,9},{13,17},{21,25},... | collective-permute-start | bytes 685064 | tf_op jit(solution)/shard_map/ppermute | solution.py:628
  9.3 0.2 collective-permute-done.1.ytwo
  9.4 0.0 collective-permute-done.yone
  9.4 0.3 pack_late.1
  9.8 4.2 %collective-permute-start.4 = (f32[32,256]{1,0:T(8,128)S(1)}, f32[32,256]{1,0:T(8,128)S(1)}, u32[]{:S(2)}, u32[]{:S(2)}) collective-permute-start(f32[32,256]{1,0:T(8,128)S(1)} %get-tuple-element.47), channel_id=1, source_target_pairs={{0,4},{8,12},{16,20},{24,28},{4,0},{12,8},{20,16},{28,24},{1,5},{9... | collective-permute-start | bytes 98312 | tf_op jit(solution)/shard_map/ppermute | solution.py:628
  14.0 0.7 %collective-permute-start.5 = (f32[32,256]{1,0:T(8,128)S(1)}, f32[32,256]{1,0:T(8,128)S(1)}, u32[]{:S(2)}, u32[]{:S(2)}) collective-permute-start(f32[32,256]{1,0:T(8,128)S(1)} %get-tuple-element.48), channel_id=1, source_target_pairs={{4,8},{12,16},{20,24},{8,4},{16,12},{24,20},{5,9},{13,17},{21,25},... | collective-permute-start | bytes 98312 | tf_op jit(solution)/shard_map/ppermute | solution.py:628
  14.6 0.8 %own.1 = (f32[8,40,256]{2,1,0:T(8,128)S(1)}, f32[8,40,256]{2,1,0:T(8,128)S(1)}, f32[8,40,256]{2,1,0:T(8,128)S(1)}, f32[8,40,256]{2,1,0:T(8,128)S(1)}, f32[8,40,2...) custom-call(f32[8,32,256]{2,1,0:T(8,128)S(1)} %get-tuple-element.28., ...), custom_call_target="tpu_custom_call" | custom-call | tf_op jit(solution)/shard_map/own/pallas_call | solution.py:309
  15.5 0.4 %inside.1 = (f32[8,40,256]{2,1,0:T(8,128)S(1)}, f32[8,40,256]{2,1,0:T(8,128)S(1)}, f32[8,8,256]{2,1,0:T(8,128)S(1)}) custom-call(f32[8,40,256]{2,1,0:T(8,128)S(1)} %get-tuple-element.34.d_s, f32[8,40,256]{2,1,0:T(8,128)S(1)} %get-tuple-element.35.s_s, f32[8,40,256]{2,1,0:T(8,128)S(1)} %get-tuple-element.36.fx, f32[8,40,256]{2,1,0:T(8,128)S(1)} %get-tuple-element.37.gx, ...), custom_call_target="tpu_custom_call" | custom-call | flops 4194304 | bytes 8388608 | tf_op jit(solution)/shard_map/inside/pallas_call | solution.py:381
  15.9 0.0 collective-permute-done.3.xone
  15.9 0.0 collective-permute-done.2.xtwo
  15.9 2.1 %collective-permute-done.4.ctwo = f32[32,256]{1,0:T(8,128)S(1)} collective-permute-done((f32[32,256]{1,0:T(8,128)S(1)}, f32[32,256]{1,0:T(8,128)S(1)}, u32[]{:S(2)}, u32[]{:S(2)}) %collective-permute-start.4) | collective-permute-done | bytes 32800 | tf_op jit(solution)/shard_map/ppermute | solution.py:628
  18.0 0.0 collective-permute-done.5.cone
  18.0 1.0 %finish.1 = (f32[8,32,256]{2,1,0:T(8,128)S(1)}, f32[8,32,256]{2,1,0:T(8,128)S(1)}, f32[10,40,256]{2,1,0:T(8,128)S(1)}, f32[2,8,40,256]{3,2,1,0:T(8,128)S(1)}, f32[32,1,128]{2,1,0:T(1,128)S(1)}) custom-call(f32[8,40,256]{2,1,0:T(8,128)S(1)} %get-tuple-element.33.u_s, f32[8,40,256]{2,1,0:T(8,128)S(1)} %get-tuple-element.34.d_s, ...), custom_call_target="tpu_custom_call" | custom-call | tf_op jit(solution)/shard_map/finish/pallas_call | solution.py:532
  19.0 13.0 %all_to_all.5 = f32[32,1,128]{2,1,0:T(1,128)S(1)} all-to-all(f32[32,1,128]{2,1,0:T(1,128)S(1)} %get-tuple-element.49), channel_id=1, replica_groups=mesh['gx'=8,'gy'=4] {'gx','gy'}, dimensions={0} | all-to-all | bytes 32768 | tf_op jit(solution)/shard_map/all_to_all | solution.py:647
  32.0 1.1 %combine.1 = (f32[8,32,256]{2,1,0:T(8,128)}, f32[8,32,256]{2,1,0:T(8,128)}) custom-call(f32[32,128]{1,0:T(8,128)S(1)} %bitcast.1, f32[8,32,256]{2,1,0:T(8,128)S(1)} %get-tuple-element.30.source, f32[8,40,256]{2,1,0:T(8,128)S(1)} %get-tuple-element.43.p1.p1_in, f32[8,40,256]{2,1,0:T(8,128)S(1)} %get-tuple-element.44.p2_in, ...), custom_call_target="tpu_custom_call" | custom-call | tf_op jit(solution)/shard_map/combine/pallas_call | solution.py:611
  (1 shorter events, 0.0 us)
Async XLA Ops:
  1.8 7.6 %collective-permute-start = (f32[3,9,8,256]{3,2,1,0:T(8,128)S(1)}, f32[3,9,8,256]{3,2,1,0:T(8,128)S(1)}, u32[]{:S(2)}, u32[]{:S(2)}) collective-permute-start(f32[3,9,8,256]{3,2,1,0:T(8,128)S(1)} %get-tuple-element.31), channel_id=1, source_target_pairs={{1,2},{2,1},{5,6},{6,5},{9,10},{10,9},{13,14},{14,13},{17,18},{18,... | collective-permute-start | bytes 663560 | tf_op jit(solution)/shard_map/ppermute | solution.py:628
  2.8 13.2 %collective-permute-start.2 = (f32[225,256]{1,0:T(8,128)S(1)}, f32[225,256]{1,0:T(8,128)S(1)}, u32[]{:S(2)}, u32[]{:S(2)}) collective-permute-start(f32[225,256]{1,0:T(8,128)S(1)} %pack_face.2), channel_id=1, source_target_pairs={{0,4},{8,12},{16,20},{24,28},{4,0},{12,8},{20,16},{28,24},{1,5},{9... | collective-permute-start | bytes 691208 | tf_op jit(solution)/shard_map/ppermute | solution.py:628
  5.8 3.7 %collective-permute-start.1 = (f32[3,8,8,256]{3,2,1,0:T(8,128)S(1)}, f32[3,8,8,256]{3,2,1,0:T(8,128)S(1)}, u32[]{:S(2)}, u32[]{:S(2)}) collective-permute-start(f32[3,8,8,256]{3,2,1,0:T(8,128)S(1)} %get-tuple-element.32), channel_id=1, source_target_pairs={{0,1},{2,3},{1,0},{3,2},{4,5},{6,7},{5,4},{7,6},{8,9},{10,11},{9,8... | collective-permute-start | bytes 589832 | tf_op jit(solution)/shard_map/ppermute | solution.py:628
  8.6 7.3 %collective-permute-start.3 = (f32[223,256]{1,0:T(8,128)S(1)}, f32[223,256]{1,0:T(8,128)S(1)}, u32[]{:S(2)}, u32[]{:S(2)}) collective-permute-start(f32[223,256]{1,0:T(8,128)S(1)} %pack_face.3), channel_id=1, source_target_pairs={{4,8},{12,16},{20,24},{8,4},{16,12},{24,20},{5,9},{13,17},{21,25},... | collective-permute-start | bytes 685064 | tf_op jit(solution)/shard_map/ppermute | solution.py:628
  9.8 8.3 %collective-permute-start.4 = (f32[32,256]{1,0:T(8,128)S(1)}, f32[32,256]{1,0:T(8,128)S(1)}, u32[]{:S(2)}, u32[]{:S(2)}) collective-permute-start(f32[32,256]{1,0:T(8,128)S(1)} %get-tuple-element.47), channel_id=1, source_target_pairs={{0,4},{8,12},{16,20},{24,28},{4,0},{12,8},{20,16},{28,24},{1,5},{9... | collective-permute-start | bytes 98312 | tf_op jit(solution)/shard_map/ppermute | solution.py:628
  14.0 4.1 %collective-permute-start.5 = (f32[32,256]{1,0:T(8,128)S(1)}, f32[32,256]{1,0:T(8,128)S(1)}, u32[]{:S(2)}, u32[]{:S(2)}) collective-permute-start(f32[32,256]{1,0:T(8,128)S(1)} %get-tuple-element.48), channel_id=1, source_target_pairs={{4,8},{12,16},{20,24},{8,4},{16,12},{24,20},{5,9},{13,17},{21,25},... | collective-permute-start | bytes 98312 | tf_op jit(solution)/shard_map/ppermute | solution.py:628
where the time goes:
time: 33.3 us; the launch traced here: 33.1 us
  blocking collectives  13 us (39%)
  starting transfers between devices  11.8 us (35%)
  Pallas kernels  5.29 us (16%)
  waiting for transfers between devices  2.27 us (7%)
  between operations  0.73 us (2%)
    all_to_all x1, blocking collectives, local(): moments = lax.all_to_all(moments, ('gx', 'gy'), 0, 0, tiled=True)  13 us
    ppermute x6, starting transfers between devices, swap(): return lax.ppermute(cells, axis, pairs + [(j, i) for i, j in pairs])  11.8 us
    ppermute x6, waiting for transfers between devices, swap(): return lax.ppermute(cells, axis, pairs + [(j, i) for i, j in pairs])  2.27 us
    pallas_call x1, Pallas kernels, pack(): pl.pallas_call(pack_kernel, out_shape=(f32(nx, ny, nz),) * 3, in_specs=[p...  1.14 us
    pallas_call x1, Pallas kernels, combine(): pl.pallas_call(combine_kernel, out_shape=(f32(nx, ny, nz),) * 2, in_specs...  1.07 us
    pallas_call x1, Pallas kernels, finish(): pl.pallas_call(finish_kernel, out_shape=(f32(nx, ny, nz), f32(nx, ny, nz)...  0.99 us
    pallas_call x1, Pallas kernels, own(): pl.pallas_call(own_kernel, out_shape=(f32(nx, ny + 2 * W, nz),) * 11, in_...  0.85 us
  transfers between devices with their start and end apart: 6, of which 2 were waited for; matrix products, arithmetic and copies ran while one was open for 0% of the time, Pallas kernels for 6%

commit v1 on v0

--- a/solution.py
+++ b/solution.py
@@ -12,7 +12,7 @@
 W = 2 * ITERS
 F32 = jnp.float32
 LANES = 128
-YROWS = (8, 8)
+TILE = 8
 VMEM = pl.BlockSpec(memory_space=pltpu.VMEM)
 
 
@@ -120,16 +120,19 @@
     nx, ny, nz = conc.shape
     flip = low_first("gy")
     for k, ref in enumerate((conc, diff, source)):
-        for out, n, head in ((yone, YROWS[0], flip), (ytwo, YROWS[1], ~flip)):
-            out[k, 0:nx] = jnp.where(head, ref[:, 0:n, :], ref[:, ny - n : ny, :])
-        yone[k, nx] = jnp.zeros((YROWS[0], nz), F32)
+        yone[k] = jnp.where(flip, ref[:, 0:TILE, :], ref[:, ny - TILE : ny, :])
+        for x in range(nx):
+            at = (k * nx + x) * TILE
+            end = min(at + TILE, ytwo.shape[0])
+            ytwo[at : at + W] = jnp.where(flip, ref[x, ny - W : ny], ref[x, 0:W])
+            ytwo[at + W : end] = jnp.zeros((end - at - W, nz), F32)
 
 
 def pack_rows(conc, diff, source):
     nx, ny, nz = conc.shape
     return pl.pallas_call(
         pack_rows_kernel,
-        out_shape=(f32(3, nx + 1, YROWS[0], nz), f32(3, nx, YROWS[1], nz)),
+        out_shape=(f32(3, nx, TILE, nz), f32(3 * nx * TILE - 1, nz)),
         in_specs=[VMEM] * 3,
         out_specs=(VMEM,) * 2,
         compiler_params=params(),
@@ -139,9 +142,14 @@
 
 def rows_beside(yone, ytwo, k, x):
     flip = low_first("gy")
-    one, two = (slice(n - W, n) for n in YROWS)
-    below = jnp.where(flip, yone[k, x, one], ytwo[k, x, two])
-    return below, jnp.where(flip, ytwo[k, x, 0:W], yone[k, x, 0:W])
+    nx = yone.shape[1]
+    if isinstance(x, slice):
+        starts = [(k * nx + q) * TILE for q in range(nx)]
+        two = jnp.stack([ytwo[at : at + W] for at in starts])
+    else:
+        two = ytwo[pl.ds(pl.multiple_of((k * nx + x) * TILE, TILE), W)]
+    below = jnp.where(flip, yone[k, x, TILE - W :], two)
+    return below, jnp.where(flip, two, yone[k, x, 0:W])
 
 
 def in_plane_adjoint(v, fy, gy, fz, gz):
@@ -192,7 +200,7 @@
 
 
 def face_rows(first_swap, ny):
-    return FIELDS * ny + (-1 if first_swap else 1)
+    return FIELDS * ny - (1 if first_swap else 0)
 
 
 def pack_face_kernel(first_swap, conc, diff, source, slab):
@@ -202,8 +210,6 @@
     for k, v in enumerate(face_fields(u, d, s)):
         n = min(ny, slab.shape[0] - k * ny)
         slab[k * ny : k * ny + n] = v[0:n]
-    if not first_swap:
-        slab[FIELDS * ny :] = jnp.zeros((1, nz), F32)
 
 
 def pack_face(first_swap, conc, diff, source):

time: 33.3 us -> 33.2 us (level)
  no operation moved by 1% of the time
where the time goes in v1:
time: 33.2 us; the launch traced here: 33 us
  blocking collectives  13 us (39%)
  starting transfers between devices  11.8 us (36%)
  Pallas kernels  5.07 us (15%)
  waiting for transfers between devices  2.4 us (7%)
  between operations  0.73 us (2%)
    all_to_all x1, blocking collectives, local(): moments = lax.all_to_all(moments, ('gx', 'gy'), 0, 0, tiled=True)  13 us
    ppermute x6, starting transfers between devices, swap(): return lax.ppermute(cells, axis, pairs + [(j, i) for i, j in pairs])  11.8 us
    ppermute x6, waiting for transfers between devices, swap(): return lax.ppermute(cells, axis, pairs + [(j, i) for i, j in pairs])  2.4 us
    pallas_call x1, Pallas kernels, pack(): pl.pallas_call(pack_kernel, out_shape=(f32(nx, ny, nz),) * 3, in_specs=[p...  1.14 us
    pallas_call x1, Pallas kernels, combine(): pl.pallas_call(combine_kernel, out_shape=(f32(nx, ny, nz),) * 2, in_specs...  1.05 us
    pallas_call x1, Pallas kernels, finish(): pl.pallas_call(finish_kernel, out_shape=(f32(nx, ny, nz), f32(nx, ny, nz)...  0.9 us
    pallas_call x1, Pallas kernels, own(): pl.pallas_call(own_kernel, out_shape=(f32(nx, ny + 2 * W, nz),) * 11, in_...  0.75 us
  transfers between devices with their start and end apart: 6, of which 2 were waited for; matrix products, arithmetic and copies ran while one was open for 0% of the time, Pallas kernels for 6%

profile of v1, /device:TPU:0, one launch (start us, length us, event | category | flops | bytes accessed | tf_op | source)
XLA Modules:
  0.0 33.0 jit_solution(10166707148549655896)
XLA Ops:
  0.6 1.1 %pack.1 = (f32[8,32,256]{2,1,0:T(8,128)S(1)}, f32[8,32,256]{2,1,0:T(8,128)S(1)}, f32[8,32,256]{2,1,0:T(8,128)S(1)}) custom-call(f32[3]{0:T(128)} %kappa_in.1, f32[8,32,256]{2,1,0:T(8,128)} %conc_in.1, s32[8,32,256]{2,1,0:T(8,128)} %labels_in.1, f32[8,32,256]{2,1,0:T(8,128)} %source_in.1), custom_call_target="tpu_custom_call" | custom-call | tf_op jit(solution)/shard_map/pack/pallas_call | solution.py:104
  1.8 0.1 pack_rows.1
  1.9 0.7 %collective-permute-start = (f32[3,8,8,256]{3,2,1,0:T(8,128)S(1)}, f32[3,8,8,256]{3,2,1,0:T(8,128)S(1)}, u32[]{:S(2)}, u32[]{:S(2)}) collective-permute-start(f32[3,8,8,256]{3,2,1,0:T(8,128)S(1)} %get-tuple-element.31), channel_id=1, source_target_pairs={{1,2},{2,1},{5,6},{6,5},{9,10},{10,9},{13,14},{14,13},{17,18},{18,... | collective-permute-start | bytes 589832 | tf_op jit(solution)/shard_map/ppermute | solution.py:634
  2.5 0.2 pack_face.2
  2.8 3.0 %collective-permute-start.2 = (f32[224,256]{1,0:T(8,128)S(1)}, f32[224,256]{1,0:T(8,128)S(1)}, u32[]{:S(2)}, u32[]{:S(2)}) collective-permute-start(f32[224,256]{1,0:T(8,128)S(1)} %pack_face.2), channel_id=1, source_target_pairs={{0,4},{8,12},{16,20},{24,28},{4,0},{12,8},{20,16},{28,24},{1,5},{9... | collective-permute-start | bytes 688136 | tf_op jit(solution)/shard_map/ppermute | solution.py:634
  5.8 2.6 %collective-permute-start.1 = (f32[191,256]{1,0:T(8,128)S(1)}, f32[191,256]{1,0:T(8,128)S(1)}, u32[]{:S(2)}, u32[]{:S(2)}) collective-permute-start(f32[191,256]{1,0:T(8,128)S(1)} %get-tuple-element.32), channel_id=1, source_target_pairs={{0,1},{2,3},{1,0},{3,2},{4,5},{6,7},{5,4},{7,6},{8,9},{10,11},{9,8... | collective-permute-start | bytes 586760 | tf_op jit(solution)/shard_map/ppermute | solution.py:634
  8.4 0.2 pack_face.3
  8.6 0.7 %collective-permute-start.3 = (f32[223,256]{1,0:T(8,128)S(1)}, f32[223,256]{1,0:T(8,128)S(1)}, u32[]{:S(2)}, u32[]{:S(2)}) collective-permute-start(f32[223,256]{1,0:T(8,128)S(1)} %pack_face.3), channel_id=1, source_target_pairs={{4,8},{12,16},{20,24},{8,4},{16,12},{24,20},{5,9},{13,17},{21,25},... | collective-permute-start | bytes 685064 | tf_op jit(solution)/shard_map/ppermute | solution.py:634
  9.3 0.2 collective-permute-done.1.ytwo
  9.4 0.0 collective-permute-done.yone
  9.4 0.3 pack_late.1
  9.8 4.2 %collective-permute-start.4 = (f32[32,256]{1,0:T(8,128)S(1)}, f32[32,256]{1,0:T(8,128)S(1)}, u32[]{:S(2)}, u32[]{:S(2)}) collective-permute-start(f32[32,256]{1,0:T(8,128)S(1)} %get-tuple-element.47), channel_id=1, source_target_pairs={{0,4},{8,12},{16,20},{24,28},{4,0},{12,8},{20,16},{28,24},{1,5},{9... | collective-permute-start | bytes 98312 | tf_op jit(solution)/shard_map/ppermute | solution.py:634
  14.0 0.7 %collective-permute-start.5 = (f32[32,256]{1,0:T(8,128)S(1)}, f32[32,256]{1,0:T(8,128)S(1)}, u32[]{:S(2)}, u32[]{:S(2)}) collective-permute-start(f32[32,256]{1,0:T(8,128)S(1)} %get-tuple-element.48), channel_id=1, source_target_pairs={{4,8},{12,16},{20,24},{8,4},{16,12},{24,20},{5,9},{13,17},{21,25},... | collective-permute-start | bytes 98312 | tf_op jit(solution)/shard_map/ppermute | solution.py:634
  14.6 0.7 %own.1 = (f32[8,40,256]{2,1,0:T(8,128)S(1)}, f32[8,40,256]{2,1,0:T(8,128)S(1)}, f32[8,40,256]{2,1,0:T(8,128)S(1)}, f32[8,40,256]{2,1,0:T(8,128)S(1)}, f32[8,40,2...) custom-call(f32[8,32,256]{2,1,0:T(8,128)S(1)} %get-tuple-element.28., ...), custom_call_target="tpu_custom_call" | custom-call | tf_op jit(solution)/shard_map/own/pallas_call | solution.py:315
  15.4 0.4 %inside.1 = (f32[8,40,256]{2,1,0:T(8,128)S(1)}, f32[8,40,256]{2,1,0:T(8,128)S(1)}, f32[8,8,256]{2,1,0:T(8,128)S(1)}) custom-call(f32[8,40,256]{2,1,0:T(8,128)S(1)} %get-tuple-element.34.d_s, f32[8,40,256]{2,1,0:T(8,128)S(1)} %get-tuple-element.35.s_s, f32[8,40,256]{2,1,0:T(8,128)S(1)} %get-tuple-element.36.fx, f32[8,40,256]{2,1,0:T(8,128)S(1)} %get-tuple-element.37.gx, ...), custom_call_target="tpu_custom_call" | custom-call | flops 4194304 | bytes 8388608 | tf_op jit(solution)/shard_map/inside/pallas_call | solution.py:387
  15.8 0.0 collective-permute-done.3.xone
  15.8 0.0 collective-permute-done.2.xtwo
  15.8 2.2 %collective-permute-done.4.ctwo = f32[32,256]{1,0:T(8,128)S(1)} collective-permute-done((f32[32,256]{1,0:T(8,128)S(1)}, f32[32,256]{1,0:T(8,128)S(1)}, u32[]{:S(2)}, u32[]{:S(2)}) %collective-permute-start.4) | collective-permute-done | bytes 32800 | tf_op jit(solution)/shard_map/ppermute | solution.py:634
  18.0 0.0 collective-permute-done.5.cone
  18.0 0.9 %finish.1 = (f32[8,32,256]{2,1,0:T(8,128)S(1)}, f32[8,32,256]{2,1,0:T(8,128)S(1)}, f32[10,40,256]{2,1,0:T(8,128)S(1)}, f32[2,8,40,256]{3,2,1,0:T(8,128)S(1)}, f32[32,1,128]{2,1,0:T(1,128)S(1)}) custom-call(f32[8,40,256]{2,1,0:T(8,128)S(1)} %get-tuple-element.33.u_s, f32[8,40,256]{2,1,0:T(8,128)S(1)} %get-tuple-element.34.d_s, ...), custom_call_target="tpu_custom_call" | custom-call | tf_op jit(solution)/shard_map/finish/pallas_call | solution.py:538
  18.9 13.0 %all_to_all.5 = f32[32,1,128]{2,1,0:T(1,128)S(1)} all-to-all(f32[32,1,128]{2,1,0:T(1,128)S(1)} %get-tuple-element.49), channel_id=1, replica_groups=mesh['gx'=8,'gy'=4] {'gx','gy'}, dimensions={0} | all-to-all | bytes 32768 | tf_op jit(solution)/shard_map/all_to_all | solution.py:653
  32.0 1.0 %combine.1 = (f32[8,32,256]{2,1,0:T(8,128)}, f32[8,32,256]{2,1,0:T(8,128)}) custom-call(f32[32,128]{1,0:T(8,128)S(1)} %bitcast.1, f32[8,32,256]{2,1,0:T(8,128)S(1)} %get-tuple-element.30.source, f32[8,40,256]{2,1,0:T(8,128)S(1)} %get-tuple-element.43.p1.p1_in, f32[8,40,256]{2,1,0:T(8,128)S(1)} %get-tuple-element.44.p2_in, ...), custom_call_target="tpu_custom_call" | custom-call | tf_op jit(solution)/shard_map/combine/pallas_call | solution.py:617
Async XLA Ops:
  1.9 7.6 %collective-permute-start = (f32[3,8,8,256]{3,2,1,0:T(8,128)S(1)}, f32[3,8,8,256]{3,2,1,0:T(8,128)S(1)}, u32[]{:S(2)}, u32[]{:S(2)}) collective-permute-start(f32[3,8,8,256]{3,2,1,0:T(8,128)S(1)} %get-tuple-element.31), channel_id=1, source_target_pairs={{1,2},{2,1},{5,6},{6,5},{9,10},{10,9},{13,14},{14,13},{17,18},{18,... | collective-permute-start | bytes 589832 | tf_op jit(solution)/shard_map/ppermute | solution.py:634
  2.8 13.0 %collective-permute-start.2 = (f32[224,256]{1,0:T(8,128)S(1)}, f32[224,256]{1,0:T(8,128)S(1)}, u32[]{:S(2)}, u32[]{:S(2)}) collective-permute-start(f32[224,256]{1,0:T(8,128)S(1)} %pack_face.2), channel_id=1, source_target_pairs={{0,4},{8,12},{16,20},{24,28},{4,0},{12,8},{20,16},{28,24},{1,5},{9... | collective-permute-start | bytes 688136 | tf_op jit(solution)/shard_map/ppermute | solution.py:634
  5.8 3.7 %collective-permute-start.1 = (f32[191,256]{1,0:T(8,128)S(1)}, f32[191,256]{1,0:T(8,128)S(1)}, u32[]{:S(2)}, u32[]{:S(2)}) collective-permute-start(f32[191,256]{1,0:T(8,128)S(1)} %get-tuple-element.32), channel_id=1, source_target_pairs={{0,1},{2,3},{1,0},{3,2},{4,5},{6,7},{5,4},{7,6},{8,9},{10,11},{9,8... | collective-permute-start | bytes 586760 | tf_op jit(solution)/shard_map/ppermute | solution.py:634
  8.6 7.2 %collective-permute-start.3 = (f32[223,256]{1,0:T(8,128)S(1)}, f32[223,256]{1,0:T(8,128)S(1)}, u32[]{:S(2)}, u32[]{:S(2)}) collective-permute-start(f32[223,256]{1,0:T(8,128)S(1)} %pack_face.3), channel_id=1, source_target_pairs={{4,8},{12,16},{20,24},{8,4},{16,12},{24,20},{5,9},{13,17},{21,25},... | collective-permute-start | bytes 685064 | tf_op jit(solution)/shard_map/ppermute | solution.py:634
  9.8 8.3 %collective-permute-start.4 = (f32[32,256]{1,0:T(8,128)S(1)}, f32[32,256]{1,0:T(8,128)S(1)}, u32[]{:S(2)}, u32[]{:S(2)}) collective-permute-start(f32[32,256]{1,0:T(8,128)S(1)} %get-tuple-element.47), channel_id=1, source_target_pairs={{0,4},{8,12},{16,20},{24,28},{4,0},{12,8},{20,16},{28,24},{1,5},{9... | collective-permute-start | bytes 98312 | tf_op jit(solution)/shard_map/ppermute | solution.py:634
  14.0 4.1 %collective-permute-start.5 = (f32[32,256]{1,0:T(8,128)S(1)}, f32[32,256]{1,0:T(8,128)S(1)}, u32[]{:S(2)}, u32[]{:S(2)}) collective-permute-start(f32[32,256]{1,0:T(8,128)S(1)} %get-tuple-element.48), channel_id=1, source_target_pairs={{4,8},{12,16},{20,24},{8,4},{16,12},{24,20},{5,9},{13,17},{21,25},... | collective-permute-start | bytes 98312 | tf_op jit(solution)/shard_map/ppermute | solution.py:634

commit v2 on v0

--- a/solution.py
+++ b/solution.py
@@ -13,6 +13,7 @@
 F32 = jnp.float32
 LANES = 128
 YROWS = (8, 8)
+TILE = 8
 VMEM = pl.BlockSpec(memory_space=pltpu.VMEM)
 
 
@@ -192,7 +193,7 @@
 
 
 def face_rows(first_swap, ny):
-    return FIELDS * ny + (-1 if first_swap else 1)
+    return FIELDS * ny + (0 if first_swap else TILE)
 
 
 def pack_face_kernel(first_swap, conc, diff, source, slab):
@@ -203,7 +204,7 @@
         n = min(ny, slab.shape[0] - k * ny)
         slab[k * ny : k * ny + n] = v[0:n]
     if not first_swap:
-        slab[FIELDS * ny :] = jnp.zeros((1, nz), F32)
+        slab[FIELDS * ny :] = jnp.zeros((TILE, nz), F32)
 
 
 def pack_face(first_swap, conc, diff, source):

time: 33.3 us -> 33.3 us (level)
  no operation moved by 1% of the time
where the time goes in v2:
time: 33.3 us; the launch traced here: 33.1 us
  blocking collectives  13 us (39%)
  starting transfers between devices  11.8 us (35%)
  Pallas kernels  5.29 us (16%)
  waiting for transfers between devices  2.27 us (7%)
  between operations  0.73 us (2%)
    all_to_all x1, blocking collectives, local(): moments = lax.all_to_all(moments, ('gx', 'gy'), 0, 0, tiled=True)  13 us
    ppermute x6, starting transfers between devices, swap(): return lax.ppermute(cells, axis, pairs + [(j, i) for i, j in pairs])  11.8 us
    ppermute x6, waiting for transfers between devices, swap(): return lax.ppermute(cells, axis, pairs + [(j, i) for i, j in pairs])  2.27 us
    pallas_call x1, Pallas kernels, pack(): pl.pallas_call(pack_kernel, out_shape=(f32(nx, ny, nz),) * 3, in_specs=[p...  1.14 us
    pallas_call x1, Pallas kernels, combine(): pl.pallas_call(combine_kernel, out_shape=(f32(nx, ny, nz),) * 2, in_specs...  1.07 us
    pallas_call x1, Pallas kernels, finish(): pl.pallas_call(finish_kernel, out_shape=(f32(nx, ny, nz), f32(nx, ny, nz)...  0.99 us
    pallas_call x1, Pallas kernels, own(): pl.pallas_call(own_kernel, out_shape=(f32(nx, ny + 2 * W, nz),) * 11, in_...  0.85 us
  transfers between devices with their start and end apart: 6, of which 2 were waited for; matrix products, arithmetic and copies ran while one was open for 0% of the time, Pallas kernels for 6%

profile of v2, /device:TPU:0, one launch (start us, length us, event | category | flops | bytes accessed | tf_op | source)
XLA Modules:
  0.0 33.1 jit_solution(16971239962293314793)
XLA Ops:
  0.6 1.1 %pack.1 = (f32[8,32,256]{2,1,0:T(8,128)S(1)}, f32[8,32,256]{2,1,0:T(8,128)S(1)}, f32[8,32,256]{2,1,0:T(8,128)S(1)}) custom-call(f32[3]{0:T(128)} %kappa_in.1, f32[8,32,256]{2,1,0:T(8,128)} %conc_in.1, s32[8,32,256]{2,1,0:T(8,128)} %labels_in.1, f32[8,32,256]{2,1,0:T(8,128)} %source_in.1), custom_call_target="tpu_custom_call" | custom-call | tf_op jit(solution)/shard_map/pack/pallas_call | solution.py:105
  1.8 0.7 %collective-permute-start = (f32[3,9,8,256]{3,2,1,0:T(8,128)S(1)}, f32[3,9,8,256]{3,2,1,0:T(8,128)S(1)}, u32[]{:S(2)}, u32[]{:S(2)}) collective-permute-start(f32[3,9,8,256]{3,2,1,0:T(8,128)S(1)} %get-tuple-element.31), channel_id=1, source_target_pairs={{1,2},{2,1},{5,6},{6,5},{9,10},{10,9},{13,14},{14,13},{17,18},{18,... | collective-permute-start | bytes 663560 | tf_op jit(solution)/shard_map/ppermute | solution.py:629
  2.5 0.2 pack_face.2
  2.8 3.0 %collective-permute-start.2 = (f32[232,256]{1,0:T(8,128)S(1)}, f32[232,256]{1,0:T(8,128)S(1)}, u32[]{:S(2)}, u32[]{:S(2)}) collective-permute-start(f32[232,256]{1,0:T(8,128)S(1)} %pack_face.2), channel_id=1, source_target_pairs={{0,4},{8,12},{16,20},{24,28},{4,0},{12,8},{20,16},{28,24},{1,5},{9... | collective-permute-start | bytes 712712 | tf_op jit(solution)/shard_map/ppermute | solution.py:629
  5.8 2.6 %collective-permute-start.1 = (f32[3,8,8,256]{3,2,1,0:T(8,128)S(1)}, f32[3,8,8,256]{3,2,1,0:T(8,128)S(1)}, u32[]{:S(2)}, u32[]{:S(2)}) collective-permute-start(f32[3,8,8,256]{3,2,1,0:T(8,128)S(1)} %get-tuple-element.32), channel_id=1, source_target_pairs={{0,1},{2,3},{1,0},{3,2},{4,5},{6,7},{5,4},{7,6},{8,9},{10,11},{9,8... | collective-permute-start | bytes 589832 | tf_op jit(solution)/shard_map/ppermute | solution.py:629
  8.4 0.2 pack_face.3
  8.6 0.7 %collective-permute-start.3 = (f32[224,256]{1,0:T(8,128)S(1)}, f32[224,256]{1,0:T(8,128)S(1)}, u32[]{:S(2)}, u32[]{:S(2)}) collective-permute-start(f32[224,256]{1,0:T(8,128)S(1)} %pack_face.3), channel_id=1, source_target_pairs={{4,8},{12,16},{20,24},{8,4},{16,12},{24,20},{5,9},{13,17},{21,25},... | collective-permute-start | bytes 688136 | tf_op jit(solution)/shard_map/ppermute | solution.py:629
  9.3 0.2 collective-permute-done.1.ytwo
  9.4 0.0 collective-permute-done.yone
  9.4 0.3 pack_late.1
  9.8 4.2 %collective-permute-start.4 = (f32[32,256]{1,0:T(8,128)S(1)}, f32[32,256]{1,0:T(8,128)S(1)}, u32[]{:S(2)}, u32[]{:S(2)}) collective-permute-start(f32[32,256]{1,0:T(8,128)S(1)} %get-tuple-element.47), channel_id=1, source_target_pairs={{0,4},{8,12},{16,20},{24,28},{4,0},{12,8},{20,16},{28,24},{1,5},{9... | collective-permute-start | bytes 98312 | tf_op jit(solution)/shard_map/ppermute | solution.py:629
  14.0 0.7 %collective-permute-start.5 = (f32[32,256]{1,0:T(8,128)S(1)}, f32[32,256]{1,0:T(8,128)S(1)}, u32[]{:S(2)}, u32[]{:S(2)}) collective-permute-start(f32[32,256]{1,0:T(8,128)S(1)} %get-tuple-element.48), channel_id=1, source_target_pairs={{4,8},{12,16},{20,24},{8,4},{16,12},{24,20},{5,9},{13,17},{21,25},... | collective-permute-start | bytes 98312 | tf_op jit(solution)/shard_map/ppermute | solution.py:629
  14.6 0.8 %own.1 = (f32[8,40,256]{2,1,0:T(8,128)S(1)}, f32[8,40,256]{2,1,0:T(8,128)S(1)}, f32[8,40,256]{2,1,0:T(8,128)S(1)}, f32[8,40,256]{2,1,0:T(8,128)S(1)}, f32[8,40,2...) custom-call(f32[8,32,256]{2,1,0:T(8,128)S(1)} %get-tuple-element.28., ...), custom_call_target="tpu_custom_call" | custom-call | tf_op jit(solution)/shard_map/own/pallas_call | solution.py:310
  15.5 0.4 %inside.1 = (f32[8,40,256]{2,1,0:T(8,128)S(1)}, f32[8,40,256]{2,1,0:T(8,128)S(1)}, f32[8,8,256]{2,1,0:T(8,128)S(1)}) custom-call(f32[8,40,256]{2,1,0:T(8,128)S(1)} %get-tuple-element.34.d_s, f32[8,40,256]{2,1,0:T(8,128)S(1)} %get-tuple-element.35.s_s, f32[8,40,256]{2,1,0:T(8,128)S(1)} %get-tuple-element.36.fx, f32[8,40,256]{2,1,0:T(8,128)S(1)} %get-tuple-element.37.gx, ...), custom_call_target="tpu_custom_call" | custom-call | flops 4194304 | bytes 8388608 | tf_op jit(solution)/shard_map/inside/pallas_call | solution.py:382
  15.9 0.0 collective-permute-done.3.xone
  15.9 0.0 collective-permute-done.2.xtwo
  15.9 2.1 %collective-permute-done.4.ctwo = f32[32,256]{1,0:T(8,128)S(1)} collective-permute-done((f32[32,256]{1,0:T(8,128)S(1)}, f32[32,256]{1,0:T(8,128)S(1)}, u32[]{:S(2)}, u32[]{:S(2)}) %collective-permute-start.4) | collective-permute-done | bytes 32800 | tf_op jit(solution)/shard_map/ppermute | solution.py:629
  18.0 0.0 collective-permute-done.5.cone
  18.0 1.0 %finish.1 = (f32[8,32,256]{2,1,0:T(8,128)S(1)}, f32[8,32,256]{2,1,0:T(8,128)S(1)}, f32[10,40,256]{2,1,0:T(8,128)S(1)}, f32[2,8,40,256]{3,2,1,0:T(8,128)S(1)}, f32[32,1,128]{2,1,0:T(1,128)S(1)}) custom-call(f32[8,40,256]{2,1,0:T(8,128)S(1)} %get-tuple-element.33.u_s, f32[8,40,256]{2,1,0:T(8,128)S(1)} %get-tuple-element.34.d_s, ...), custom_call_target="tpu_custom_call" | custom-call | tf_op jit(solution)/shard_map/finish/pallas_call | solution.py:533
  19.0 13.0 %all_to_all.5 = f32[32,1,128]{2,1,0:T(1,128)S(1)} all-to-all(f32[32,1,128]{2,1,0:T(1,128)S(1)} %get-tuple-element.49), channel_id=1, replica_groups=mesh['gx'=8,'gy'=4] {'gx','gy'}, dimensions={0} | all-to-all | bytes 32768 | tf_op jit(solution)/shard_map/all_to_all | solution.py:648
  32.0 1.1 %combine.1 = (f32[8,32,256]{2,1,0:T(8,128)}, f32[8,32,256]{2,1,0:T(8,128)}) custom-call(f32[32,128]{1,0:T(8,128)S(1)} %bitcast.1, f32[8,32,256]{2,1,0:T(8,128)S(1)} %get-tuple-element.30.source, f32[8,40,256]{2,1,0:T(8,128)S(1)} %get-tuple-element.43.p1.p1_in, f32[8,40,256]{2,1,0:T(8,128)S(1)} %get-tuple-element.44.p2_in, ...), custom_call_target="tpu_custom_call" | custom-call | tf_op jit(solution)/shard_map/combine/pallas_call | solution.py:612
  (1 shorter events, 0.0 us)
Async XLA Ops:
  1.8 7.6 %collective-permute-start = (f32[3,9,8,256]{3,2,1,0:T(8,128)S(1)}, f32[3,9,8,256]{3,2,1,0:T(8,128)S(1)}, u32[]{:S(2)}, u32[]{:S(2)}) collective-permute-start(f32[3,9,8,256]{3,2,1,0:T(8,128)S(1)} %get-tuple-element.31), channel_id=1, source_target_pairs={{1,2},{2,1},{5,6},{6,5},{9,10},{10,9},{13,14},{14,13},{17,18},{18,... | collective-permute-start | bytes 663560 | tf_op jit(solution)/shard_map/ppermute | solution.py:629
  2.8 13.2 %collective-permute-start.2 = (f32[232,256]{1,0:T(8,128)S(1)}, f32[232,256]{1,0:T(8,128)S(1)}, u32[]{:S(2)}, u32[]{:S(2)}) collective-permute-start(f32[232,256]{1,0:T(8,128)S(1)} %pack_face.2), channel_id=1, source_target_pairs={{0,4},{8,12},{16,20},{24,28},{4,0},{12,8},{20,16},{28,24},{1,5},{9... | collective-permute-start | bytes 712712 | tf_op jit(solution)/shard_map/ppermute | solution.py:629
  5.8 3.7 %collective-permute-start.1 = (f32[3,8,8,256]{3,2,1,0:T(8,128)S(1)}, f32[3,8,8,256]{3,2,1,0:T(8,128)S(1)}, u32[]{:S(2)}, u32[]{:S(2)}) collective-permute-start(f32[3,8,8,256]{3,2,1,0:T(8,128)S(1)} %get-tuple-element.32), channel_id=1, source_target_pairs={{0,1},{2,3},{1,0},{3,2},{4,5},{6,7},{5,4},{7,6},{8,9},{10,11},{9,8... | collective-permute-start | bytes 589832 | tf_op jit(solution)/shard_map/ppermute | solution.py:629
  8.6 7.3 %collective-permute-start.3 = (f32[224,256]{1,0:T(8,128)S(1)}, f32[224,256]{1,0:T(8,128)S(1)}, u32[]{:S(2)}, u32[]{:S(2)}) collective-permute-start(f32[224,256]{1,0:T(8,128)S(1)} %pack_face.3), channel_id=1, source_target_pairs={{4,8},{12,16},{20,24},{8,4},{16,12},{24,20},{5,9},{13,17},{21,25},... | collective-permute-start | bytes 688136 | tf_op jit(solution)/shard_map/ppermute | solution.py:629
  9.8 8.3 %collective-permute-start.4 = (f32[32,256]{1,0:T(8,128)S(1)}, f32[32,256]{1,0:T(8,128)S(1)}, u32[]{:S(2)}, u32[]{:S(2)}) collective-permute-start(f32[32,256]{1,0:T(8,128)S(1)} %get-tuple-element.47), channel_id=1, source_target_pairs={{0,4},{8,12},{16,20},{24,28},{4,0},{12,8},{20,16},{28,24},{1,5},{9... | collective-permute-start | bytes 98312 | tf_op jit(solution)/shard_map/ppermute | solution.py:629
  14.0 4.1 %collective-permute-start.5 = (f32[32,256]{1,0:T(8,128)S(1)}, f32[32,256]{1,0:T(8,128)S(1)}, u32[]{:S(2)}, u32[]{:S(2)}) collective-permute-start(f32[32,256]{1,0:T(8,128)S(1)} %get-tuple-element.48), channel_id=1, source_target_pairs={{4,8},{12,16},{20,24},{8,4},{16,12},{24,20},{5,9},{13,17},{21,25},... | collective-permute-start | bytes 98312 | tf_op jit(solution)/shard_map/ppermute | solution.py:629

commit v3 on v2

--- a/solution.py
+++ b/solution.py
@@ -12,7 +12,6 @@
 W = 2 * ITERS
 F32 = jnp.float32
 LANES = 128
-YROWS = (8, 8)
 TILE = 8
 VMEM = pl.BlockSpec(memory_space=pltpu.VMEM)
 
@@ -120,17 +119,21 @@
 def pack_rows_kernel(conc, diff, source, yone, ytwo):
     nx, ny, nz = conc.shape
     flip = low_first("gy")
-    for k, ref in enumerate((conc, diff, source)):
-        for out, n, head in ((yone, YROWS[0], flip), (ytwo, YROWS[1], ~flip)):
-            out[k, 0:nx] = jnp.where(head, ref[:, 0:n, :], ref[:, ny - n : ny, :])
-        yone[k, nx] = jnp.zeros((YROWS[0], nz), F32)
+    for out, head in ((yone, flip), (ytwo, ~flip)):
+        for k, ref in enumerate((conc, diff, source)):
+            for x in range(nx):
+                at = (k * nx + x) * TILE
+                out[at : at + W] = jnp.where(head, ref[x, 0:W], ref[x, ny - W : ny])
+                out[at + W : at + TILE] = jnp.zeros((TILE - W, nz), F32)
+    yone[3 * nx * TILE :] = jnp.zeros((TILE, nz), F32)
 
 
 def pack_rows(conc, diff, source):
     nx, ny, nz = conc.shape
+    rows = 3 * nx * TILE
     return pl.pallas_call(
         pack_rows_kernel,
-        out_shape=(f32(3, nx + 1, YROWS[0], nz), f32(3, nx, YROWS[1], nz)),
+        out_shape=(f32(rows + TILE, nz), f32(rows, nz)),
         in_specs=[VMEM] * 3,
         out_specs=(VMEM,) * 2,
         compiler_params=params(),
@@ -140,9 +143,16 @@
 
 def rows_beside(yone, ytwo, k, x):
     flip = low_first("gy")
-    one, two = (slice(n - W, n) for n in YROWS)
-    below = jnp.where(flip, yone[k, x, one], ytwo[k, x, two])
-    return below, jnp.where(flip, ytwo[k, x, 0:W], yone[k, x, 0:W])
+    nx = ytwo.shape[0] // (3 * TILE)
+
+    def lead(ref):
+        if isinstance(x, slice):
+            starts = [(k * nx + q) * TILE for q in range(nx)]
+            return jnp.stack([ref[at : at + W] for at in starts])
+        return ref[pl.ds(pl.multiple_of((k * nx + x) * TILE, TILE), W)]
+
+    one, two = lead(yone), lead(ytwo)
+    return jnp.where(flip, one, two), jnp.where(flip, two, one)
 
 
 def in_plane_adjoint(v, fy, gy, fz, gz):

time: 33.3 us -> 33.3 us (level)
  no operation moved by 1% of the time
where the time goes in v3:
time: 33.3 us; the launch traced here: 33.1 us
  blocking collectives  13 us (39%)
  starting transfers between devices  11.8 us (35%)
  Pallas kernels  5.29 us (16%)
  waiting for transfers between devices  2.33 us (7%)
  between operations  0.72 us (2%)
    all_to_all x1, blocking collectives, local(): moments = lax.all_to_all(moments, ('gx', 'gy'), 0, 0, tiled=True)  13 us
    ppermute x6, starting transfers between devices, swap(): return lax.ppermute(cells, axis, pairs + [(j, i) for i, j in pairs])  11.8 us
    ppermute x6, waiting for transfers between devices, swap(): return lax.ppermute(cells, axis, pairs + [(j, i) for i, j in pairs])  2.33 us
    pallas_call x1, Pallas kernels, pack(): pl.pallas_call(pack_kernel, out_shape=(f32(nx, ny, nz),) * 3, in_specs=[p...  1.14 us
    pallas_call x1, Pallas kernels, combine(): pl.pallas_call(combine_kernel, out_shape=(f32(nx, ny, nz),) * 2, in_specs...  1.07 us
    pallas_call x1, Pallas kernels, finish(): pl.pallas_call(finish_kernel, out_shape=(f32(nx, ny, nz), f32(nx, ny, nz)...  0.99 us
    pallas_call x1, Pallas kernels, own(): pl.pallas_call(own_kernel, out_shape=(f32(nx, ny + 2 * W, nz),) * 11, in_...  0.82 us
  transfers between devices with their start and end apart: 6, of which 2 were waited for; matrix products, arithmetic and copies ran while one was open for 0% of the time, Pallas kernels for 6%

profile of v3, /device:TPU:0, one launch (start us, length us, event | category | flops | bytes accessed | tf_op | source)
XLA Modules:
  0.0 33.1 jit_solution(10142455895129976609)
XLA Ops:
  0.6 1.1 %pack.1 = (f32[8,32,256]{2,1,0:T(8,128)S(1)}, f32[8,32,256]{2,1,0:T(8,128)S(1)}, f32[8,32,256]{2,1,0:T(8,128)S(1)}) custom-call(f32[3]{0:T(128)} %kappa_in.1, f32[8,32,256]{2,1,0:T(8,128)} %conc_in.1, s32[8,32,256]{2,1,0:T(8,128)} %labels_in.1, f32[8,32,256]{2,1,0:T(8,128)} %source_in.1), custom_call_target="tpu_custom_call" | custom-call | tf_op jit(solution)/shard_map/pack/pallas_call | solution.py:104
  1.8 0.1 pack_rows.1
  1.9 0.7 %collective-permute-start = (f32[200,256]{1,0:T(8,128)S(1)}, f32[200,256]{1,0:T(8,128)S(1)}, u32[]{:S(2)}, u32[]{:S(2)}) collective-permute-start(f32[200,256]{1,0:T(8,128)S(1)} %get-tuple-element.31), channel_id=1, source_target_pairs={{1,2},{2,1},{5,6},{6,5},{9,10},{10,9},{13,14},{14,13},{17,18},{18,... | collective-permute-start | bytes 614408 | tf_op jit(solution)/shard_map/ppermute | solution.py:639
  2.5 0.2 pack_face.2
  2.8 3.0 %collective-permute-start.2 = (f32[232,256]{1,0:T(8,128)S(1)}, f32[232,256]{1,0:T(8,128)S(1)}, u32[]{:S(2)}, u32[]{:S(2)}) collective-permute-start(f32[232,256]{1,0:T(8,128)S(1)} %pack_face.2), channel_id=1, source_target_pairs={{0,4},{8,12},{16,20},{24,28},{4,0},{12,8},{20,16},{28,24},{1,5},{9... | collective-permute-start | bytes 712712 | tf_op jit(solution)/shard_map/ppermute | solution.py:639
  5.8 2.6 %collective-permute-start.1 = (f32[192,256]{1,0:T(8,128)S(1)}, f32[192,256]{1,0:T(8,128)S(1)}, u32[]{:S(2)}, u32[]{:S(2)}) collective-permute-start(f32[192,256]{1,0:T(8,128)S(1)} %get-tuple-element.32), channel_id=1, source_target_pairs={{0,1},{2,3},{1,0},{3,2},{4,5},{6,7},{5,4},{7,6},{8,9},{10,11},{9,8... | collective-permute-start | bytes 589832 | tf_op jit(solution)/shard_map/ppermute | solution.py:639
  8.4 0.2 pack_face.3
  8.6 0.7 %collective-permute-start.3 = (f32[224,256]{1,0:T(8,128)S(1)}, f32[224,256]{1,0:T(8,128)S(1)}, u32[]{:S(2)}, u32[]{:S(2)}) collective-permute-start(f32[224,256]{1,0:T(8,128)S(1)} %pack_face.3), channel_id=1, source_target_pairs={{4,8},{12,16},{20,24},{8,4},{16,12},{24,20},{5,9},{13,17},{21,25},... | collective-permute-start | bytes 688136 | tf_op jit(solution)/shard_map/ppermute | solution.py:639
  9.3 0.2 collective-permute-done.1.ytwo
  9.5 0.0 collective-permute-done.yone
  9.5 0.3 pack_late.1
  9.8 4.2 %collective-permute-start.4 = (f32[32,256]{1,0:T(8,128)S(1)}, f32[32,256]{1,0:T(8,128)S(1)}, u32[]{:S(2)}, u32[]{:S(2)}) collective-permute-start(f32[32,256]{1,0:T(8,128)S(1)} %get-tuple-element.47), channel_id=1, source_target_pairs={{0,4},{8,12},{16,20},{24,28},{4,0},{12,8},{20,16},{28,24},{1,5},{9... | collective-permute-start | bytes 98312 | tf_op jit(solution)/shard_map/ppermute | solution.py:639
  14.0 0.7 %collective-permute-start.5 = (f32[32,256]{1,0:T(8,128)S(1)}, f32[32,256]{1,0:T(8,128)S(1)}, u32[]{:S(2)}, u32[]{:S(2)}) collective-permute-start(f32[32,256]{1,0:T(8,128)S(1)} %get-tuple-element.48), channel_id=1, source_target_pairs={{4,8},{12,16},{20,24},{8,4},{16,12},{24,20},{5,9},{13,17},{21,25},... | collective-permute-start | bytes 98312 | tf_op jit(solution)/shard_map/ppermute | solution.py:639
  14.6 0.8 %own.1 = (f32[8,40,256]{2,1,0:T(8,128)S(1)}, f32[8,40,256]{2,1,0:T(8,128)S(1)}, f32[8,40,256]{2,1,0:T(8,128)S(1)}, f32[8,40,256]{2,1,0:T(8,128)S(1)}, f32[8,40,2...) custom-call(f32[8,32,256]{2,1,0:T(8,128)S(1)} %get-tuple-element.28., ...), custom_call_target="tpu_custom_call" | custom-call | tf_op jit(solution)/shard_map/own/pallas_call | solution.py:320
  15.5 0.4 %inside.1 = (f32[8,40,256]{2,1,0:T(8,128)S(1)}, f32[8,40,256]{2,1,0:T(8,128)S(1)}, f32[8,8,256]{2,1,0:T(8,128)S(1)}) custom-call(f32[8,40,256]{2,1,0:T(8,128)S(1)} %get-tuple-element.34.d_s, f32[8,40,256]{2,1,0:T(8,128)S(1)} %get-tuple-element.35.s_s, f32[8,40,256]{2,1,0:T(8,128)S(1)} %get-tuple-element.36.fx, f32[8,40,256]{2,1,0:T(8,128)S(1)} %get-tuple-element.37.gx, ...), custom_call_target="tpu_custom_call" | custom-call | flops 4194304 | bytes 8388608 | tf_op jit(solution)/shard_map/inside/pallas_call | solution.py:392
  15.9 0.0 collective-permute-done.3.xone
  15.9 2.2 %collective-permute-done.4.ctwo = f32[32,256]{1,0:T(8,128)S(1)} collective-permute-done((f32[32,256]{1,0:T(8,128)S(1)}, f32[32,256]{1,0:T(8,128)S(1)}, u32[]{:S(2)}, u32[]{:S(2)}) %collective-permute-start.4) | collective-permute-done | bytes 32800 | tf_op jit(solution)/shard_map/ppermute | solution.py:639
  18.1 0.0 collective-permute-done.5.cone
  18.1 0.0 collective-permute-done.2.xtwo
  18.1 1.0 %finish.1 = (f32[8,32,256]{2,1,0:T(8,128)S(1)}, f32[8,32,256]{2,1,0:T(8,128)S(1)}, f32[10,40,256]{2,1,0:T(8,128)S(1)}, f32[2,8,40,256]{3,2,1,0:T(8,128)S(1)}, f32[32,1,128]{2,1,0:T(1,128)S(1)}) custom-call(f32[8,40,256]{2,1,0:T(8,128)S(1)} %get-tuple-element.33.u_s, f32[8,40,256]{2,1,0:T(8,128)S(1)} %get-tuple-element.34.d_s, ...), custom_call_target="tpu_custom_call" | custom-call | tf_op jit(solution)/shard_map/finish/pallas_call | solution.py:543
  19.1 13.0 %all_to_all.5 = f32[32,1,128]{2,1,0:T(1,128)S(1)} all-to-all(f32[32,1,128]{2,1,0:T(1,128)S(1)} %get-tuple-element.49), channel_id=1, replica_groups=mesh['gx'=8,'gy'=4] {'gx','gy'}, dimensions={0} | all-to-all | bytes 32768 | tf_op jit(solution)/shard_map/all_to_all | solution.py:658
  32.0 1.1 %combine.1 = (f32[8,32,256]{2,1,0:T(8,128)}, f32[8,32,256]{2,1,0:T(8,128)}) custom-call(f32[32,128]{1,0:T(8,128)S(1)} %bitcast.1, f32[8,32,256]{2,1,0:T(8,128)S(1)} %get-tuple-element.30.source, f32[8,40,256]{2,1,0:T(8,128)S(1)} %get-tuple-element.43.p1.p1_in, f32[8,40,256]{2,1,0:T(8,128)S(1)} %get-tuple-element.44.p2_in, ...), custom_call_target="tpu_custom_call" | custom-call | tf_op jit(solution)/shard_map/combine/pallas_call | solution.py:622
Async XLA Ops:
  1.9 7.6 %collective-permute-start = (f32[200,256]{1,0:T(8,128)S(1)}, f32[200,256]{1,0:T(8,128)S(1)}, u32[]{:S(2)}, u32[]{:S(2)}) collective-permute-start(f32[200,256]{1,0:T(8,128)S(1)} %get-tuple-element.31), channel_id=1, source_target_pairs={{1,2},{2,1},{5,6},{6,5},{9,10},{10,9},{13,14},{14,13},{17,18},{18,... | collective-permute-start | bytes 614408 | tf_op jit(solution)/shard_map/ppermute | solution.py:639
  2.8 15.3 %collective-permute-start.2 = (f32[232,256]{1,0:T(8,128)S(1)}, f32[232,256]{1,0:T(8,128)S(1)}, u32[]{:S(2)}, u32[]{:S(2)}) collective-permute-start(f32[232,256]{1,0:T(8,128)S(1)} %pack_face.2), channel_id=1, source_target_pairs={{0,4},{8,12},{16,20},{24,28},{4,0},{12,8},{20,16},{28,24},{1,5},{9... | collective-permute-start | bytes 712712 | tf_op jit(solution)/shard_map/ppermute | solution.py:639
  5.8 3.7 %collective-permute-start.1 = (f32[192,256]{1,0:T(8,128)S(1)}, f32[192,256]{1,0:T(8,128)S(1)}, u32[]{:S(2)}, u32[]{:S(2)}) collective-permute-start(f32[192,256]{1,0:T(8,128)S(1)} %get-tuple-element.32), channel_id=1, source_target_pairs={{0,1},{2,3},{1,0},{3,2},{4,5},{6,7},{5,4},{7,6},{8,9},{10,11},{9,8... | collective-permute-start | bytes 589832 | tf_op jit(solution)/shard_map/ppermute | solution.py:639
  8.6 7.3 %collective-permute-start.3 = (f32[224,256]{1,0:T(8,128)S(1)}, f32[224,256]{1,0:T(8,128)S(1)}, u32[]{:S(2)}, u32[]{:S(2)}) collective-permute-start(f32[224,256]{1,0:T(8,128)S(1)} %pack_face.3), channel_id=1, source_target_pairs={{4,8},{12,16},{20,24},{8,4},{16,12},{24,20},{5,9},{13,17},{21,25},... | collective-permute-start | bytes 688136 | tf_op jit(solution)/shard_map/ppermute | solution.py:639
  9.8 8.3 %collective-permute-start.4 = (f32[32,256]{1,0:T(8,128)S(1)}, f32[32,256]{1,0:T(8,128)S(1)}, u32[]{:S(2)}, u32[]{:S(2)}) collective-permute-start(f32[32,256]{1,0:T(8,128)S(1)} %get-tuple-element.47), channel_id=1, source_target_pairs={{0,4},{8,12},{16,20},{24,28},{4,0},{12,8},{20,16},{28,24},{1,5},{9... | collective-permute-start | bytes 98312 | tf_op jit(solution)/shard_map/ppermute | solution.py:639
  14.0 4.1 %collective-permute-start.5 = (f32[32,256]{1,0:T(8,128)S(1)}, f32[32,256]{1,0:T(8,128)S(1)}, u32[]{:S(2)}, u32[]{:S(2)}) collective-permute-start(f32[32,256]{1,0:T(8,128)S(1)} %get-tuple-element.48), channel_id=1, source_target_pairs={{4,8},{12,16},{20,24},{8,4},{16,12},{24,20},{5,9},{13,17},{21,25},... | collective-permute-start | bytes 98312 | tf_op jit(solution)/shard_map/ppermute | solution.py:639
